TPU v7x, 512 devices: a whole 4x8x8 slice. The times are simulated.
512 devices in a mesh: ka: 64 (over z, x, y_lo), ta: 8 (over y_hi, core).
Axes of the slice: x: 4, y: 8 (y_hi: 4, y_lo: 2; y = y_hi * 2 + y_lo), z: 8, core: 2. Of those that a mesh axis runs over, the one named last changes fastest.
Arguments:
- green_time: bfloat16 [2048, 256, 256], P(('ta', 'ka')), parts along dimension 0, may hold values from -0.375 to 0.375
- orbitals: bfloat16 [256, 256, 512], P('ka'), may hold values from -3.296875 to 3.296875
- pair_table: int32 [256, 256], P(None, 'ka'), may hold values from 0 to 255, as said below
- pair_momenta: int32 [2], replicated, may hold values from 0 to 255
- owner_rows: int32 [512], replicated, may hold values from 0 to 511, each once
Outputs:
- bubble: float32 [4096, 2, 512], P(('ta', 'ka')), parts along dimension 0
There are 8 independent parts, one for each index of `ta`. A program takes and returns all parts, laid end to end along the dimension named above; an argument that names none is the same for every part. Nothing has to cross between parts.
Inputs may be any that keep to these rules, and one draw needn't show every extreme that they name: The momenta form a 4 x 4 x (16) periodic lattice listed in an order drawn from the seed; row a of pair_table gives, for each k, the index of momentum a minus momentum k, so every row is a permutation of 0 to 255.
All inputs are finite; a program needn't handle non-finite values.
Results may differ from a plain program's by a relative error of at most 0.0057.
Values may be sent and summed in bfloat16 or wider, within the bound.
A program may use at most 64 MiB of HBM per device.

v0:
```python
import jax
import jax.numpy as jnp
from jax import lax
from jax.sharding import PartitionSpec as P


def per_device(green_time, orbitals, pair_table, pair_momenta, owner_rows):
    orbitals_owned = jnp.take(orbitals, owner_rows, axis=2)
    half_product = jnp.einsum(
        "kij,kjp->kip", green_time, orbitals, preferred_element_type=jnp.float32
    ).astype(jnp.bfloat16)
    projected = jnp.einsum(
        "kia,kip->kap", orbitals_owned, half_product, preferred_element_type=jnp.float32
    ).astype(jnp.bfloat16)
    local_pairs = jnp.take(pair_table, pair_momenta, axis=0)
    partners = lax.all_gather(local_pairs, "ka", axis=1, tiled=True)
    inverse_count = 1.0 / partners.shape[1]
    spread = lax.all_to_all(projected, "ka", split_axis=1, concat_axis=0, tiled=True)
    partner_blocks = jnp.take(spread, partners, axis=0)
    returned = lax.all_to_all(partner_blocks, "ka", split_axis=1, concat_axis=2, tiled=True)
    return lax.psum_scatter(
        jnp.einsum("kac,qkac->aqc", projected, returned, preferred_element_type=jnp.float32)
        * inverse_count,
        "ka",
        scatter_dimension=0,
        tiled=True,
    )


def solution(mesh):
    return jax.shard_map(
        per_device,
        mesh=mesh,
        in_specs=(P(("ta", "ka"), None, None), P("ka", None, None), P(None, "ka"), P(), P()),
        out_specs=P(("ta", "ka"), None, None),
        check_vma=False,
    )
```

profile of v0, /device:TPU:16, one launch (start us, length us, event | category | flops | bytes accessed | tf_op | source)
XLA Modules:
  0.0 922.7 jit_solution(13758151225031022009)
XLA Ops:
  6.5 0.0 copy-start
  6.5 0.7 compare_select_fusion.1
  7.3 0.7 compare_and_fusion.1
  8.0 1.7 copy.32
  9.7 2.4 gather_fusion.1
  12.1 2.7 select_bitcast_fusion
  14.7 0.0 copy-done
  14.7 4.5 bitcast_convert_fusion
  19.2 0.0 copy-start.2
  19.2 0.0 copy-start.3
  19.2 2.9 copy.34
  22.1 14.8 %all-to-all-start = ((bf16[4,512,512]{2,0,1:T(4,128)(2,1)}), bf16[4,512,512]{2,0,1:T(4,128)(2,1)S(1)}, u32[]{:S(2)}, u32[]{:S(2)}) async-start(bf16[4,512,512]{2,0,1:T(4,128)(2,1)} %copy.34), calls=%async_computation | async-start | bytes 4194304 | tf_op jit(solution)/shard_map/all_to_all | solution.py:18
  36.9 0.0 all-reduce.3.cloned.1.call-start
  37.0 0.0 copy-done.2
  37.0 0.1 copy.29
  37.1 0.0 copy-done.3
  37.2 0.6 gather_fusion
  37.8 0.1 select_bitcast_fusion.1
  37.8 173.9 %all-gather = s32[64,4,2]{1,2,0:T(2,128)S(1)} all-gather(s32[1,4,2]{1,2,0:T(2,128)S(1)} %select_bitcast_fusion.1), channel_id=1, replica_groups=mesh['ka'=64,'ta'=8] {'ka'}, dimensions={0}, use_global_device_ids=true | all-gather | bytes 2080 | tf_op jit(solution)/shard_map/all_gather | solution.py:16
  211.7 0.1 reshape.44
  211.9 0.2 copy.31
  212.1 0.0 all-to-all-done
  212.1 0.4 copy.61
  212.5 0.3 copy.36
  212.8 3.5 gather_fusion.2
  216.3 2.6 copy_select_fusion
  218.9 0.0 copy-start.1
  218.9 73.9 %all_to_all.36 = bf16[2,256,8,512]{3,2,0,1:T(8,128)(2,1)S(1)} all-to-all(bf16[2,256,8,512]{3,2,0,1:T(8,128)(2,1)S(1)} %copy_select_fusion), channel_id=1, replica_groups=mesh['ka'=64,'ta'=8] {'ka'}, dimensions={1} | all-to-all | bytes 8388608 | tf_op jit(solution)/shard_map/all_to_all | solution.py:20
  292.7 0.0 copy-done.1
  292.7 1.2 multiply_reduce_fusion
  293.9 0.2 broadcast_multiply_fusion
  294.1 2.9 copy.60
  297.1 0.0 all-reduce.3.cloned.1.call-update
  297.1 1.3 dynamic-slice
  299.0 615.5 %all-reduce.3.cloned.1.call-done = f32[512,2,512]{2,1,0:T(2,128)} async-done(((f32[512,2,512]{2,1,0:T(2,128)}), f32[512,2,512]{2,1,0:T(2,128)}) %all-reduce.3.cloned.1.call-update) | async-done | bytes 2097168
  914.5 1.4 constant_dynamic-slice_fusion
  (9 shorter events, 0.1 us)
Async XLA Ops:
  6.5 8.2 copy-start
  19.2 17.8 %copy-start.2 = (s32[256,4]{0,1:T(4,128)S(1)}, s32[256,4]{0,1:T(4,128)}, u32[]{:S(2)}) copy-start(s32[256,4]{0,1:T(4,128)} %param.7) | copy-start | bytes 12292
  19.2 18.0 %copy-start.3 = (s32[2]{0:T(128)S(1)}, s32[2]{0:T(128)}, u32[]{:S(2)}) copy-start(s32[2]{0:T(128)} %param.8) | copy-start | bytes 28
  22.1 189.9 %all-to-all-start = ((bf16[4,512,512]{2,0,1:T(4,128)(2,1)}), bf16[4,512,512]{2,0,1:T(4,128)(2,1)S(1)}, u32[]{:S(2)}, u32[]{:S(2)}) async-start(bf16[4,512,512]{2,0,1:T(4,128)(2,1)} %copy.34), calls=%async_computation | async-start | bytes 4194304 | tf_op jit(solution)/shard_map/all_to_all | solution.py:18
  36.9 877.5 %all-reduce.3.cloned.1.call-start = ((), (), s32[]{:S(2)}) async-start(), calls=%async_computation.2 | async-start | bytes 4194304
  218.9 73.9 %copy-start.1 = (f32[512,512,4]{1,0,2:T(8,128)S(1)}, f32[512,512,4]{1,0,2:T(8,128)}, u32[]{:S(2)}) copy-start(f32[512,512,4]{1,0,2:T(8,128)} %get-tuple-element.5) | copy-start | bytes 12582916
Sparse Core Ops, SparseCore 0:
  297.2 617.2 all-reduce.2
where the time goes:
time: 923 us
  waiting for transfers between devices  615 us (67%)
  blocking collectives  248 us (27%)
  local copies, waits for them, and re-layouts  17.7 us (2%)
  starting transfers between devices  14.8 us (2%)
  between operations  14.2 us (2%)
    unnamed x2, waiting for transfers between devices  615 us
    all_gather x1, blocking collectives, per_device(): partners = lax.all_gather(local_pairs, 'ka', axis=1, tiled=True)  174 us
    all_to_all x1, blocking collectives, per_device(): lax.all_to_all(partner_blocks, 'ka', split_axis=1, concat_axis=2, tiled=T...  73.9 us
  transfers between devices with their start and end apart: 2, of which 1 were waited for; matrix products, arithmetic and copies ran while one was open for 0% of the time, Pallas kernels for 0%

commit v1 on v0

v1 whole, which is shorter than its diff:
```python
import functools

import jax
import jax.numpy as jnp
from jax import lax
from jax.experimental import pallas as pl
from jax.experimental.pallas import tpu as pltpu
from jax.sharding import PartitionSpec as P

MESH = pl.DeviceIdType.MESH


def kernel(
    n, q_ref, green_ref, orb_ref, table_ref, owner_ref, out_ref,
    green, orb, select, owned, send, recv, pair_send, pair_recv, pairs,
    load_sem, send_sem, recv_sem, pair_send_sem, pair_recv_sem, local_sem,
):
    me = lax.axis_index("ka")
    per, norb, npts = green.shape[0], orb.shape[1], orb.shape[2]
    nq = q_ref.shape[0]
    rows = npts // n
    half = npts // 2

    load_green = pltpu.make_async_copy(green_ref, green, load_sem.at[0])
    load_orb = pltpu.make_async_copy(orb_ref, orb, load_sem.at[1])
    load_orb.start()
    load_green.start()

    barrier = pltpu.get_barrier_semaphore()

    @pl.loop(1, n)
    def _(step):
        peer = lax.rem(me + step, n)
        pl.semaphore_signal(barrier, inc=1, device_id={"ka": peer}, device_id_type=MESH)

    for q in range(nq):
        rows_of_table = lax.broadcasted_iota(jnp.int32, table_ref.shape, 0)
        chosen = jnp.where(rows_of_table == q_ref[q], table_ref[...], 0)
        pair_send[0, q : q + 1, 0:per] = jnp.sum(chosen, axis=0, keepdims=True)

    owner_columns = jnp.transpose(
        jnp.broadcast_to(owner_ref[...].astype(jnp.float32), (128, npts))
    )
    for tile in range(npts // 128):
        points = (lax.broadcasted_iota(jnp.int32, (npts, 128), 1) + tile * 128).astype(jnp.float32)
        select[:, tile * 128 : (tile + 1) * 128] = jnp.where(
            owner_columns == points, 1.0, 0.0
        ).astype(jnp.bfloat16)

    load_orb.wait()
    load_green.wait()
    for k in range(per):
        owned[...] = lax.dot_general(
            select[...], orb[k], (((1,), (1,)), ((), ())), preferred_element_type=jnp.float32
        ).astype(jnp.bfloat16)
        half_product = jnp.dot(
            green[k], orb[k], preferred_element_type=jnp.float32
        ).astype(jnp.bfloat16)
        projected = jnp.dot(owned[...], half_product, preferred_element_type=jnp.float32)
        projected = projected.reshape(n, rows, npts)
        send[:, k] = jnp.concatenate(
            [projected[:, :, :half], projected[:, :, half:]], axis=1
        ).astype(jnp.bfloat16)

    pl.semaphore_wait(barrier, n - 1)

    def block_copy(step):
        peer = lax.rem(me + step, n)
        return pltpu.make_async_remote_copy(
            src_ref=send.at[peer],
            dst_ref=recv.at[pl.ds(me * per, per)],
            send_sem=send_sem.at[step],
            recv_sem=recv_sem.at[step],
            device_id={"ka": peer},
            device_id_type=MESH,
        )

    def pair_copy(step):
        peer = lax.rem(me + step, n)
        return pltpu.make_async_remote_copy(
            src_ref=pair_send.at[0],
            dst_ref=pair_recv.at[me],
            send_sem=pair_send_sem.at[step],
            recv_sem=pair_recv_sem.at[step],
            device_id={"ka": peer},
            device_id_type=MESH,
        )

    @pl.loop(1, n)
    def _(step):
        pair_copy(step).start()

    @pl.loop(1, n)
    def _(step):
        block_copy(step).start()

    own = pltpu.make_async_copy(send.at[me], recv.at[pl.ds(me * per, per)], local_sem.at[0])
    own.start()
    own_pair = pltpu.make_async_copy(pair_send.at[0], pair_recv.at[me], local_sem.at[1])
    own_pair.start()
    own.wait()
    own_pair.wait()

    @pl.loop(1, n)
    def _(step):
        pair_copy(step).wait()

    to_scalar = pltpu.make_async_copy(pair_recv, pairs, local_sem.at[2])
    to_scalar.start()
    to_scalar.wait()

    @pl.loop(1, n)
    def _(step):
        block_copy(step).wait()

    def add(device, totals):
        totals = list(totals)
        for j in range(per):
            mine = recv[device * per + j].astype(jnp.float32)
            for q in range(nq):
                partner = recv[pairs[device, q, j]].astype(jnp.float32)
                totals[q] = totals[q] + mine * partner
        return tuple(totals)

    zero = jnp.zeros(recv.shape[1:], jnp.float32)
    totals = lax.fori_loop(0, n, add, (zero,) * nq)
    for q in range(nq):
        scaled = totals[q] * (1.0 / (n * per))
        out_ref[:, q * npts : q * npts + half] = scaled[:rows]
        out_ref[:, q * npts + half : (q + 1) * npts] = scaled[rows:]


def solution(mesh):
    n = mesh.shape["ka"]

    def per_device(green_time, orbitals, pair_table, pair_momenta, owner_rows):
        per, norb, npts = orbitals.shape
        nq = pair_momenta.shape[0]
        rows = npts // n
        bf16, i32 = jnp.bfloat16, jnp.int32
        out = pl.pallas_call(
            functools.partial(kernel, n),
            out_shape=jax.ShapeDtypeStruct((rows, nq * npts), jnp.float32),
            in_specs=[
                pl.BlockSpec(memory_space=pltpu.SMEM),
                pl.BlockSpec(memory_space=pl.ANY),
                pl.BlockSpec(memory_space=pl.ANY),
                pl.BlockSpec(memory_space=pltpu.VMEM),
                pl.BlockSpec(memory_space=pltpu.VMEM),
            ],
            out_specs=pl.BlockSpec(memory_space=pltpu.VMEM),
            scratch_shapes=[
                pltpu.VMEM((per, norb, norb), bf16),
                pltpu.VMEM((per, norb, npts), bf16),
                pltpu.VMEM((npts, npts), bf16),
                pltpu.VMEM((npts, norb), bf16),
                pltpu.VMEM((n, per, 2 * rows, npts // 2), bf16),
                pltpu.VMEM((n * per, 2 * rows, npts // 2), bf16),
                pltpu.VMEM((1, nq, 128), i32),
                pltpu.VMEM((n, nq, 128), i32),
                pltpu.SMEM((n, nq, 128), i32),
                pltpu.SemaphoreType.DMA((2,)),
                pltpu.SemaphoreType.DMA((n,)),
                pltpu.SemaphoreType.DMA((n,)),
                pltpu.SemaphoreType.DMA((n,)),
                pltpu.SemaphoreType.DMA((n,)),
                pltpu.SemaphoreType.DMA((3,)),
            ],
            compiler_params=pltpu.CompilerParams(
                collective_id=0, has_side_effects=True, vmem_limit_bytes=32 * 1024 * 1024
            ),
            cost_estimate=pl.CostEstimate(
                flops=2 * per * npts * (norb * norb + npts * norb * 2),
                bytes_accessed=2 * per * norb * (norb + npts),
                transcendentals=0,
            ),
        )(pair_momenta, green_time, orbitals, pair_table, owner_rows.reshape(1, npts))
        return out.reshape(rows, nq, npts)

    return jax.shard_map(
        per_device,
        mesh=mesh,
        in_specs=(P(("ta", "ka"), None, None), P("ka", None, None), P(None, "ka"), P(), P()),
        out_specs=P(("ta", "ka"), None, None),
        check_vma=False,
    )
```

time: 923 us -> 74.5 us (0.08)
  the two profiles are of different devices: /device:TPU:16 before, /device:TPU:46 now
where the time goes in v1:
time: 74.5 us; the launch traced here: 74.2 us
  Pallas kernels  70.4 us (94%)
  local copies, waits for them, and re-layouts  3.75 us (5%)
    pallas_call x1, Pallas kernels, per_device(): pl.pallas_call(functools.partial(kernel, n), out_shape=jax.ShapeDtypeStru...  70.4 us
    unnamed x9, local copies, waits for them, and re-layouts  3.11 us

profile of v1, /device:TPU:46, one launch (start us, length us, event | category | flops | bytes accessed | tf_op | source)
XLA Modules:
  0.0 74.2 jit_solution(12904057266548838292)
XLA Ops:
  0.0 0.0 copy-start.2
  0.0 0.0 copy-start.3
  0.0 0.8 %copy.6.table_ref = s32[256,4]{1,0:T(8,128)S(1)} copy(s32[256,4]{0,1:T(4,128)} %param.7) | data formatting | bytes 8192 | tf_op args[2]
  0.9 0.0 copy-done.2
  0.9 0.0 copy-done.3
  0.9 0.0 copy-start
  0.9 1.2 %copy-done = bf16[4,256,512]{2,1,0:T(8,128)(2,1)S(1)} copy-done((bf16[4,256,512]{2,1,0:T(8,128)(2,1)S(1)}, bf16[4,256,512]{2,1,0:T(8,128)(2,1)}, u32[]{:S(2)}) %copy-start) | copy-done | bytes 1048600
  2.1 0.0 copy-start.1
  2.1 1.0 %copy-done.1 = bf16[4,256,256]{2,1,0:T(8,128)(2,1)S(1)} copy-done((bf16[4,256,256]{2,1,0:T(8,128)(2,1)S(1)}, bf16[4,256,256]{2,1,0:T(8,128)(2,1)}, u32[]{:S(2)}) %copy-start.1) | copy-done | bytes 524312
  3.1 70.4 %shard_map.55 = f32[8,1024]{1,0:T(8,128)S(1)} custom-call(s32[2]{0:T(128)S(1)} %copy-done.3, bf16[4,256,256]{2,1,0:T(8,128)(2,1)S(1)} %copy-done.1, bf16[4,256,512]{2,1,0:T(8,128)(2,1)S(1)} %copy-done, s32[256,4]{1,0:T(8,128)S(1)} %copy.6.table_ref, s32[1,512]{1,0:T(1,128)S(1)} %bitcast.3), custom_call_target="tpu_custom_call" | custom-call | flops 1342177280 | bytes 1572864 | tf_op jit(solution)/shard_map/pallas_call | solution.py:141
  73.6 0.6 copy.7
Async XLA Ops:
  0.0 0.9 %copy-start.2 = (s32[512]{0:T(512)S(1)}, s32[512]{0:T(512)}, u32[]{:S(2)}) copy-start(s32[512]{0:T(512)} %param.9) | copy-start | bytes 6148
  0.0 0.9 %copy-start.3 = (s32[2]{0:T(128)S(1)}, s32[2]{0:T(128)}, u32[]{:S(2)}) copy-start(s32[2]{0:T(128)} %q_ref.1) | copy-start | bytes 28
  0.9 1.2 %copy-start = (bf16[4,256,512]{2,1,0:T(8,128)(2,1)S(1)}, bf16[4,256,512]{2,1,0:T(8,128)(2,1)}, u32[]{:S(2)}) copy-start(bf16[4,256,512]{2,1,0:T(8,128)(2,1)} %orb_ref.1) | copy-start | bytes 3145732
  2.1 1.0 %copy-start.1 = (bf16[4,256,256]{2,1,0:T(8,128)(2,1)S(1)}, bf16[4,256,256]{2,1,0:T(8,128)(2,1)}, u32[]{:S(2)}) copy-start(bf16[4,256,256]{2,1,0:T(8,128)(2,1)} %green_ref.1) | copy-start | bytes 1572868

commit v2 on v1

v2 whole, which is shorter than its diff:
```python
import functools

import jax
import jax.numpy as jnp
from jax import lax
from jax.experimental import pallas as pl
from jax.experimental.pallas import tpu as pltpu
from jax.sharding import PartitionSpec as P

MESH = pl.DeviceIdType.MESH
PLANE = 8
LANES = 128


def kernel(
    n, q_hbm, green_hbm, orb_hbm, table_hbm, owner_hbm, out_ref,
    q_ref, green, orb, table, owner, select, owned, send, recv,
    plane_send, plane_recv, line_send, line_recv, pairs,
    load_sem, send_sem, recv_sem, plane_send_sem, plane_recv_sem, line_send_sem, line_recv_sem, local_sem,
):
    me = lax.axis_index("ka")
    line, spot = me // PLANE, me % PLANE
    lines = n // PLANE
    per, norb, npts = orb.shape
    nq = q_ref.shape[0]
    rows = npts // n
    half = npts // 2

    barrier = pltpu.get_barrier_semaphore()

    @pl.loop(1, n)
    def _(step):
        peer = lax.rem(me + step, n)
        pl.semaphore_signal(barrier, inc=1, device_id={"ka": peer}, device_id_type=MESH)

    loads = [
        pltpu.make_async_copy(source, held, load_sem.at[i])
        for i, (source, held) in enumerate(
            ((owner_hbm, owner), (q_hbm, q_ref), (table_hbm, table), (orb_hbm, orb), (green_hbm, green))
        )
    ]
    for load in loads:
        load.start()
    for load in loads[:3]:
        load.wait()

    owner_columns = jnp.transpose(
        jnp.broadcast_to(owner[...].astype(jnp.float32), (LANES, npts))
    )
    for tile in range(npts // LANES):
        points = lax.broadcasted_iota(jnp.int32, (npts, LANES), 1) + tile * LANES
        select[:, tile * LANES : (tile + 1) * LANES] = jnp.where(
            owner_columns == points.astype(jnp.float32), 1.0, 0.0
        ).astype(jnp.bfloat16)

    table_columns = lax.broadcasted_iota(jnp.int32, table.shape, 1)
    lane = lax.broadcasted_iota(jnp.int32, (per, LANES), 1)
    which = lax.broadcasted_iota(jnp.int32, (per, LANES), 0)
    placed = jnp.zeros((per, LANES), jnp.int32)
    for q in range(nq):
        chosen = jnp.where(table_columns == q_ref[q], table[...], 0)
        partner = jnp.sum(chosen, axis=1, keepdims=True)
        placed += jnp.where(lane == (spot * nq + q) * per + which, partner, 0)
    plane_send[0] = jnp.sum(placed, axis=0, keepdims=True)

    for load in loads[3:]:
        load.wait()
    for k in range(per):
        owned[...] = lax.dot_general(
            select[...], orb[k], (((1,), (1,)), ((), ())), preferred_element_type=jnp.float32
        ).astype(jnp.bfloat16)
        half_product = jnp.dot(
            green[k], orb[k], preferred_element_type=jnp.float32
        ).astype(jnp.bfloat16)
        projected = jnp.dot(owned[...], half_product, preferred_element_type=jnp.float32)
        projected = projected.reshape(n, rows, npts)
        send[:, k] = jnp.concatenate(
            [projected[:, :, :half], projected[:, :, half:]], axis=1
        ).astype(jnp.bfloat16)

    pl.semaphore_wait(barrier, n - 1)

    def block_copy(step):
        peer = lax.rem(line + step % lines, lines) * PLANE + lax.rem(spot + step // lines, PLANE)
        return pltpu.make_async_remote_copy(
            src_ref=send.at[peer],
            dst_ref=recv.at[pl.ds(me * per, per)],
            send_sem=send_sem.at[step],
            recv_sem=recv_sem.at[step],
            device_id={"ka": peer},
            device_id_type=MESH,
        )

    def plane_copy(step):
        return pltpu.make_async_remote_copy(
            src_ref=plane_send.at[0],
            dst_ref=plane_recv.at[spot],
            send_sem=plane_send_sem.at[step],
            recv_sem=plane_recv_sem.at[step],
            device_id={"ka": line * PLANE + lax.rem(spot + step, PLANE)},
            device_id_type=MESH,
        )

    def line_copy(step):
        return pltpu.make_async_remote_copy(
            src_ref=line_send.at[0],
            dst_ref=line_recv.at[line],
            send_sem=line_send_sem.at[step],
            recv_sem=line_recv_sem.at[step],
            device_id={"ka": lax.rem(line + step, lines) * PLANE + spot},
            device_id_type=MESH,
        )

    @pl.loop(1, PLANE)
    def _(step):
        plane_copy(step).start()

    @pl.loop(1, n // 2)
    def _(step):
        block_copy(step).start()

    own = pltpu.make_async_copy(send.at[me], recv.at[pl.ds(me * per, per)], local_sem.at[0])
    own.start()
    plane_own = pltpu.make_async_copy(plane_send.at[0], plane_recv.at[spot], local_sem.at[1])
    plane_own.start()
    plane_own.wait()

    @pl.loop(1, PLANE)
    def _(step):
        plane_copy(step).wait()

    line_send[0] = jnp.sum(plane_recv[...], axis=0)

    @pl.loop(1, lines)
    def _(step):
        line_copy(step).start()

    line_own = pltpu.make_async_copy(line_send.at[0], line_recv.at[line], local_sem.at[2])
    line_own.start()

    @pl.loop(n // 2, n)
    def _(step):
        block_copy(step).start()

    own.wait()
    line_own.wait()

    @pl.loop(1, lines)
    def _(step):
        line_copy(step).wait()

    to_scalar = pltpu.make_async_copy(line_recv, pairs, local_sem.at[3])
    to_scalar.start()
    to_scalar.wait()

    @pl.loop(1, n)
    def _(step):
        block_copy(step).wait()

    def add(device, totals):
        totals = list(totals)
        for j in range(per):
            mine = recv[device * per + j].astype(jnp.float32)
            for q in range(nq):
                at = pairs[device // PLANE, 0, (device % PLANE * nq + q) * per + j]
                totals[q] = totals[q] + mine * recv[at].astype(jnp.float32)
        return tuple(totals)

    zero = jnp.zeros(recv.shape[1:], jnp.float32)
    totals = lax.fori_loop(0, n, add, (zero,) * nq, unroll=4)
    for q in range(nq):
        scaled = totals[q] * (1.0 / (n * per))
        out_ref[:, q * npts : q * npts + half] = scaled[:rows]
        out_ref[:, q * npts + half : (q + 1) * npts] = scaled[rows:]


def solution(mesh):
    n = mesh.shape["ka"]

    def per_device(green_time, orbitals, pair_table, pair_momenta, owner_rows):
        per, norb, npts = orbitals.shape
        nq = pair_momenta.shape[0]
        rows = npts // n
        bf16, i32 = jnp.bfloat16, jnp.int32
        dma = pltpu.SemaphoreType.DMA
        out = pl.pallas_call(
            functools.partial(kernel, n),
            out_shape=jax.ShapeDtypeStruct((rows, nq * npts), jnp.float32),
            in_specs=[pl.BlockSpec(memory_space=pltpu.HBM)] * 5,
            out_specs=pl.BlockSpec(memory_space=pltpu.VMEM),
            scratch_shapes=[
                pltpu.SMEM((nq,), i32),
                pltpu.VMEM((per, norb, norb), bf16),
                pltpu.VMEM((per, norb, npts), bf16),
                pltpu.VMEM((per, n * per), i32),
                pltpu.VMEM((1, npts), i32),
                pltpu.VMEM((npts, npts), bf16),
                pltpu.VMEM((npts, norb), bf16),
                pltpu.VMEM((n, per, 2 * rows, npts // 2), bf16),
                pltpu.VMEM((n * per, 2 * rows, npts // 2), bf16),
                pltpu.VMEM((1, 1, LANES), i32),
                pltpu.VMEM((PLANE, 1, LANES), i32),
                pltpu.VMEM((1, 1, LANES), i32),
                pltpu.VMEM((n // PLANE, 1, LANES), i32),
                pltpu.SMEM((n // PLANE, 1, LANES), i32),
                dma((5,)),
                dma((n,)),
                dma((n,)),
                dma((PLANE,)),
                dma((PLANE,)),
                dma((n // PLANE,)),
                dma((n // PLANE,)),
                dma((4,)),
            ],
            compiler_params=pltpu.CompilerParams(
                collective_id=0, has_side_effects=True, vmem_limit_bytes=56 * 1024 * 1024
            ),
            cost_estimate=pl.CostEstimate(
                flops=2 * per * npts * (norb * norb + npts * norb * 2),
                bytes_accessed=2 * per * norb * (norb + npts),
                transcendentals=0,
            ),
        )(pair_momenta, green_time, orbitals, pair_table.T, owner_rows.reshape(1, npts))
        return out.reshape(rows, nq, npts)

    return jax.shard_map(
        per_device,
        mesh=mesh,
        in_specs=(P(("ta", "ka"), None, None), P("ka", None, None), P(None, "ka"), P(), P()),
        out_specs=P(("ta", "ka"), None, None),
        check_vma=False,
    )
```

time: 74.5 us -> 67.4 us (0.905)
  the two profiles are of different devices: /device:TPU:46 before, /device:TPU:16 now
where the time goes in v2:
time: 67.4 us; the launch traced here: 67.2 us
  Pallas kernels  65.8 us (98%)
  local copies, waits for them, and re-layouts  1.4 us (2%)
    pallas_call x1, Pallas kernels, per_device(): pl.pallas_call(functools.partial(kernel, n), out_shape=jax.ShapeDtypeStru...  65.8 us
    reshape x1, local copies, waits for them, and re-layouts, per_device(): return out.reshape(rows, nq, npts)  1.4 us

profile of v2, /device:TPU:16, one launch (start us, length us, event | category | flops | bytes accessed | tf_op | source)
XLA Modules:
  0.0 67.2 jit_solution(1265211561398638706)
XLA Ops:
  0.0 65.8 %shard_map.55 = f32[8,1024]{1,0:T(8,128)} custom-call(s32[2]{0:T(128)} %q_hbm.1, bf16[4,256,256]{2,1,0:T(8,128)(2,1)} %green_hbm.1, bf16[4,256,512]{2,1,0:T(8,128)(2,1)} %orb_hbm.1, s32[4,256]{1,0:T(4,128)} %bitcast.4, s32[1,512]{1,0:T(1,128)} %bitcast.5), custom_call_target="tpu_custom_call" | custom-call | flops 1342177280 | bytes 1572864 | tf_op jit(solution)/shard_map/pallas_call | solution.py:186
  65.8 1.4 %copy.6 = f32[8,2,512]{2,1,0:T(2,128)} copy(f32[8,2,512]{2,0,1:T(8,128)} %bitcast.3) | data formatting | bytes 65536 | tf_op jit(solution)/shard_map/reshape | solution.py:224

commit v3 on v2

--- a/solution.py
+++ b/solution.py
@@ -16,7 +16,7 @@
     n, q_hbm, green_hbm, orb_hbm, table_hbm, owner_hbm, out_ref,
     q_ref, green, orb, table, owner, select, owned, send, recv,
     plane_send, plane_recv, line_send, line_recv, pairs,
-    load_sem, send_sem, recv_sem, plane_send_sem, plane_recv_sem, line_send_sem, line_recv_sem, local_sem,
+    load_sem, send_sem, recv_sem, plane_send_sem, plane_recv_sem, line_send_sem, line_recv_sem, local_sem, ready_sem,
 ):
     me = lax.axis_index("ka")
     line, spot = me // PLANE, me % PLANE
@@ -26,12 +26,21 @@
     rows = npts // n
     half = npts // 2
 
+    def in_plane(step):
+        return {"ka": line * PLANE + lax.rem(spot + step, PLANE)}
+
+    def in_line(step):
+        return {"ka": lax.rem(line + step, lines) * PLANE + spot}
+
     barrier = pltpu.get_barrier_semaphore()
 
-    @pl.loop(1, n)
-    def _(step):
-        peer = lax.rem(me + step, n)
-        pl.semaphore_signal(barrier, inc=1, device_id={"ka": peer}, device_id_type=MESH)
+    @pl.loop(1, lines)
+    def _(step):
+        pl.semaphore_signal(barrier, inc=1, device_id=in_line(lines - step), device_id_type=MESH)
+
+    @pl.loop(1, PLANE)
+    def _(step):
+        pl.semaphore_signal(barrier, inc=1, device_id=in_plane(step), device_id_type=MESH)
 
     loads = [
         pltpu.make_async_copy(source, held, load_sem.at[i])
@@ -78,7 +87,11 @@
             [projected[:, :, :half], projected[:, :, half:]], axis=1
         ).astype(jnp.bfloat16)
 
-    pl.semaphore_wait(barrier, n - 1)
+    pl.semaphore_wait(barrier, lines - 1 + PLANE - 1)
+
+    @pl.loop(1, lines)
+    def _(step):
+        pl.semaphore_signal(ready_sem, inc=1, device_id=in_line(lines - step), device_id_type=MESH)
 
     def block_copy(step):
         peer = lax.rem(line + step % lines, lines) * PLANE + lax.rem(spot + step // lines, PLANE)
@@ -97,7 +110,7 @@
             dst_ref=plane_recv.at[spot],
             send_sem=plane_send_sem.at[step],
             recv_sem=plane_recv_sem.at[step],
-            device_id={"ka": line * PLANE + lax.rem(spot + step, PLANE)},
+            device_id=in_plane(step),
             device_id_type=MESH,
         )
 
@@ -107,17 +120,29 @@
             dst_ref=line_recv.at[line],
             send_sem=line_send_sem.at[step],
             recv_sem=line_recv_sem.at[step],
-            device_id={"ka": lax.rem(line + step, lines) * PLANE + spot},
+            device_id=in_line(step),
             device_id_type=MESH,
         )
 
+    @pl.loop(1, lines)
+    def _(step):
+        block_copy(step).start()
+
     @pl.loop(1, PLANE)
     def _(step):
         plane_copy(step).start()
-
-    @pl.loop(1, n // 2)
-    def _(step):
-        block_copy(step).start()
+        block_copy(step * lines).start()
+
+    pl.semaphore_wait(ready_sem, lines - 1)
+
+    def send_rest(first, last):
+        @pl.loop(first, last)
+        def _(turn):
+            @pl.loop(1, lines)
+            def _(step):
+                block_copy(turn * lines + step).start()
+
+    send_rest(1, PLANE // 2)
 
     own = pltpu.make_async_copy(send.at[me], recv.at[pl.ds(me * per, per)], local_sem.at[0])
     own.start()
@@ -138,9 +163,7 @@
     line_own = pltpu.make_async_copy(line_send.at[0], line_recv.at[line], local_sem.at[2])
     line_own.start()
 
-    @pl.loop(n // 2, n)
-    def _(step):
-        block_copy(step).start()
+    send_rest(PLANE // 2, PLANE)
 
     own.wait()
     line_own.wait()
@@ -211,6 +234,7 @@
                 dma((n // PLANE,)),
                 dma((n // PLANE,)),
                 dma((4,)),
+                pltpu.SemaphoreType.REGULAR,
             ],
             compiler_params=pltpu.CompilerParams(
                 collective_id=0, has_side_effects=True, vmem_limit_bytes=56 * 1024 * 1024

time: 67.4 us -> 65.2 us (0.967)
  the two profiles are of different devices: /device:TPU:16 before, /device:TPU:40 now
where the time goes in v3:
time: 65.2 us; the launch traced here: 65 us
  Pallas kernels  63.6 us (98%)
  local copies, waits for them, and re-layouts  1.4 us (2%)
    pallas_call x1, Pallas kernels, per_device(): pl.pallas_call(functools.partial(kernel, n), out_shape=jax.ShapeDtypeStru...  63.6 us
    reshape x1, local copies, waits for them, and re-layouts, per_device(): return out.reshape(rows, nq, npts)  1.4 us

profile of v3, /device:TPU:40, one launch (start us, length us, event | category | flops | bytes accessed | tf_op | source)
XLA Modules:
  0.0 65.0 jit_solution(6959724063944331666)
XLA Ops:
  0.0 63.6 %shard_map.55 = f32[8,1024]{1,0:T(8,128)} custom-call(s32[2]{0:T(128)} %q_hbm.1, bf16[4,256,256]{2,1,0:T(8,128)(2,1)} %green_hbm.1, bf16[4,256,512]{2,1,0:T(8,128)(2,1)} %orb_hbm.1, s32[4,256]{1,0:T(4,128)} %bitcast.4, s32[1,512]{1,0:T(1,128)} %bitcast.5), custom_call_target="tpu_custom_call" | custom-call | flops 1342177280 | bytes 1572864 | tf_op jit(solution)/shard_map/pallas_call | solution.py:209
  63.6 1.4 %copy.6 = f32[8,2,512]{2,1,0:T(2,128)} copy(f32[8,2,512]{2,0,1:T(8,128)} %bitcast.3) | data formatting | bytes 65536 | tf_op jit(solution)/shard_map/reshape | solution.py:248

commit v4 on v3

--- a/solution.py
+++ b/solution.py
@@ -180,21 +180,22 @@
     def _(step):
         block_copy(step).wait()
 
-    def add(device, totals):
+    def add(row, totals):
         totals = list(totals)
-        for j in range(per):
-            mine = recv[device * per + j].astype(jnp.float32)
-            for q in range(nq):
-                at = pairs[device // PLANE, 0, (device % PLANE * nq + q) * per + j]
-                totals[q] = totals[q] + mine * recv[at].astype(jnp.float32)
+        for place in range(PLANE):
+            for j in range(per):
+                mine = recv[(row * PLANE + place) * per + j].astype(jnp.float32)
+                for q in range(nq):
+                    at = pairs[row, 0, (place * nq + q) * per + j]
+                    totals[q] = totals[q] + mine * recv[at].astype(jnp.float32)
         return tuple(totals)
 
     zero = jnp.zeros(recv.shape[1:], jnp.float32)
-    totals = lax.fori_loop(0, n, add, (zero,) * nq, unroll=4)
+    totals = lax.fori_loop(0, lines, add, (zero,) * nq)
     for q in range(nq):
         scaled = totals[q] * (1.0 / (n * per))
-        out_ref[:, q * npts : q * npts + half] = scaled[:rows]
-        out_ref[:, q * npts + half : (q + 1) * npts] = scaled[rows:]
+        out_ref[:, q, :half] = scaled[:rows]
+        out_ref[:, q, half:] = scaled[rows:]
 
 
 def solution(mesh):
@@ -208,7 +209,7 @@
         dma = pltpu.SemaphoreType.DMA
         out = pl.pallas_call(
             functools.partial(kernel, n),
-            out_shape=jax.ShapeDtypeStruct((rows, nq * npts), jnp.float32),
+            out_shape=jax.ShapeDtypeStruct((rows, nq, npts), jnp.float32),
             in_specs=[pl.BlockSpec(memory_space=pltpu.HBM)] * 5,
             out_specs=pl.BlockSpec(memory_space=pltpu.VMEM),
             scratch_shapes=[
@@ -245,7 +246,7 @@
                 transcendentals=0,
             ),
         )(pair_momenta, green_time, orbitals, pair_table.T, owner_rows.reshape(1, npts))
-        return out.reshape(rows, nq, npts)
+        return out
 
     return jax.shard_map(
         per_device,

time: 65.2 us -> 64.4 us (0.988)
  Pallas kernels: 63.6 us -> 62.8 us
    reshape x1 -> x0, local copies, waits for them, and re-layouts: 1.4 us -> none  [per_device(): return out.reshape(rows, nq, npts)]
    unnamed x0 -> x1, local copies, waits for them, and re-layouts: none -> 1.38 us
    pallas_call x1, Pallas kernels: 63.6 us -> 62.8 us  [per_device(): pl.pallas_call(functools.partial(kernel, n), out_shape=jax.ShapeDtypeStru...]
where the time goes in v4:
time: 64.4 us; the launch traced here: 64.2 us
  Pallas kernels  62.8 us (98%)
  local copies, waits for them, and re-layouts  1.38 us (2%)
    pallas_call x1, Pallas kernels, per_device(): pl.pallas_call(functools.partial(kernel, n), out_shape=jax.ShapeDtypeStru...  62.8 us
    unnamed x1, local copies, waits for them, and re-layouts  1.38 us

profile of v4, /device:TPU:40, one launch (start us, length us, event | category | flops | bytes accessed | tf_op | source)
XLA Modules:
  0.0 64.2 jit_solution(6107297157377360897)
XLA Ops:
  0.0 62.8 %shard_map.55 = f32[8,2,512]{2,1,0:T(2,128)} custom-call(s32[2]{0:T(128)} %q_hbm.1, bf16[4,256,256]{2,1,0:T(8,128)(2,1)} %green_hbm.1, bf16[4,256,512]{2,1,0:T(8,128)(2,1)} %orb_hbm.1, s32[4,256]{1,0:T(4,128)} %bitcast.2, s32[1,512]{1,0:T(1,128)} %bitcast.3), custom_call_target="tpu_custom_call" | custom-call | flops 1342177280 | bytes 1572864 | tf_op jit(solution)/shard_map/pallas_call | solution.py:210
  62.8 1.4 %copy.7 = f32[8,2,512]{2,1,0:T(2,128)} copy(f32[8,2,512]{2,1,0:T(2,128)} %shard_map.55) | data formatting | bytes 65536

commit v5 on v4

--- a/solution.py
+++ b/solution.py
@@ -238,14 +238,19 @@
                 pltpu.SemaphoreType.REGULAR,
             ],
             compiler_params=pltpu.CompilerParams(
-                collective_id=0, has_side_effects=True, vmem_limit_bytes=56 * 1024 * 1024
+                collective_id=0, has_side_effects=True, vmem_limit_bytes=32 * 1024 * 1024
             ),
             cost_estimate=pl.CostEstimate(
                 flops=2 * per * npts * (norb * norb + npts * norb * 2),
                 bytes_accessed=2 * per * norb * (norb + npts),
                 transcendentals=0,
             ),
-        )(pair_momenta, green_time, orbitals, pair_table.T, owner_rows.reshape(1, npts))
+        )(
+            *(
+                pltpu.with_memory_space_constraint(operand, pltpu.HBM)
+                for operand in (pair_momenta, green_time, orbitals, pair_table.T, owner_rows.reshape(1, npts))
+            )
+        )
         return out
 
     return jax.shard_map(

time: 64.4 us -> 63 us (0.978)
  local copies, waits for them, and re-layouts: 1.38 us -> 0.62 us
    unnamed x1, local copies, waits for them, and re-layouts: 1.38 us -> 0.62 us
where the time goes in v5:
time: 63 us; the launch traced here: 62.8 us
  Pallas kernels  62.2 us (99%)
    pallas_call x1, Pallas kernels, per_device(): pl.pallas_call(functools.partial(kernel, n), out_shape=jax.ShapeDtypeStru...  62.2 us

profile of v5, /device:TPU:40, one launch (start us, length us, event | category | flops | bytes accessed | tf_op | source)
XLA Modules:
  0.0 62.8 jit_solution(7111965823401096137)
XLA Ops:
  0.0 62.2 %shard_map.55 = f32[8,2,512]{2,1,0:T(2,128)S(1)} custom-call(s32[2]{0:T(128)} %q_hbm.1, bf16[4,256,256]{2,1,0:T(8,128)(2,1)} %green_hbm.1, bf16[4,256,512]{2,1,0:T(8,128)(2,1)} %orb_hbm.1, s32[4,256]{1,0:T(4,128)} %bitcast.2, s32[1,512]{1,0:T(1,128)} %bitcast.3), custom_call_target="tpu_custom_call" | custom-call | flops 1342177280 | bytes 1572864 | tf_op jit(solution)/shard_map/pallas_call | solution.py:210
  62.2 0.6 copy.7

commit v6 on v5

--- a/solution.py
+++ b/solution.py
@@ -10,12 +10,13 @@
 MESH = pl.DeviceIdType.MESH
 PLANE = 8
 LANES = 128
+EARLY = 6
 
 
 def kernel(
     n, q_hbm, green_hbm, orb_hbm, table_hbm, owner_hbm, out_ref,
-    q_ref, green, orb, table, owner, select, owned, send, recv,
-    plane_send, plane_recv, line_send, line_recv, pairs,
+    q_ref, green, orb, table, owner, select, owned, send, early, full,
+    plane_send, plane_recv, line_send, line_recv, places, pairs,
     load_sem, send_sem, recv_sem, plane_send_sem, plane_recv_sem, line_send_sem, line_recv_sem, local_sem, ready_sem,
 ):
     me = lax.axis_index("ka")
@@ -32,6 +33,20 @@
     def in_line(step):
         return {"ka": lax.rem(line + step, lines) * PLANE + spot}
 
+    small = [
+        pltpu.make_async_copy(source, held, load_sem.at[i])
+        for i, (source, held) in enumerate(((owner_hbm, owner), (q_hbm, q_ref), (table_hbm, table)))
+    ]
+    loads = [
+        (
+            pltpu.make_async_copy(orb_hbm.at[k], orb.at[k], load_sem.at[3 + k]),
+            pltpu.make_async_copy(green_hbm.at[k], green.at[k], load_sem.at[3 + per + k]),
+        )
+        for k in range(per)
+    ]
+    for load in small + [load for both in loads for load in both]:
+        load.start()
+
     barrier = pltpu.get_barrier_semaphore()
 
     @pl.loop(1, lines)
@@ -42,15 +57,7 @@
     def _(step):
         pl.semaphore_signal(barrier, inc=1, device_id=in_plane(step), device_id_type=MESH)
 
-    loads = [
-        pltpu.make_async_copy(source, held, load_sem.at[i])
-        for i, (source, held) in enumerate(
-            ((owner_hbm, owner), (q_hbm, q_ref), (table_hbm, table), (orb_hbm, orb), (green_hbm, green))
-        )
-    ]
-    for load in loads:
-        load.start()
-    for load in loads[:3]:
+    for load in small:
         load.wait()
 
     owner_columns = jnp.transpose(
@@ -72,9 +79,9 @@
         placed += jnp.where(lane == (spot * nq + q) * per + which, partner, 0)
     plane_send[0] = jnp.sum(placed, axis=0, keepdims=True)
 
-    for load in loads[3:]:
-        load.wait()
     for k in range(per):
+        for load in loads[k]:
+            load.wait()
         owned[...] = lax.dot_general(
             select[...], orb[k], (((1,), (1,)), ((), ())), preferred_element_type=jnp.float32
         ).astype(jnp.bfloat16)
@@ -93,13 +100,17 @@
     def _(step):
         pl.semaphore_signal(ready_sem, inc=1, device_id=in_line(lines - step), device_id_type=MESH)
 
-    def block_copy(step):
-        peer = lax.rem(line + step % lines, lines) * PLANE + lax.rem(spot + step // lines, PLANE)
+    def arrival(turn, row):
+        place = (turn * lines + row) * per
+        return (early if turn < EARLY else full).at[pl.ds(place, per)]
+
+    def block_copy(turn, step):
+        peer = lax.rem(line + step, lines) * PLANE + lax.rem(spot + turn, PLANE)
         return pltpu.make_async_remote_copy(
             src_ref=send.at[peer],
-            dst_ref=recv.at[pl.ds(me * per, per)],
-            send_sem=send_sem.at[step],
-            recv_sem=recv_sem.at[step],
+            dst_ref=arrival(turn, line),
+            send_sem=send_sem.at[turn * lines + step],
+            recv_sem=recv_sem.at[turn * lines + step],
             device_id={"ka": peer},
             device_id_type=MESH,
         )
@@ -126,25 +137,23 @@
 
     @pl.loop(1, lines)
     def _(step):
-        block_copy(step).start()
-
-    @pl.loop(1, PLANE)
-    def _(step):
-        plane_copy(step).start()
-        block_copy(step * lines).start()
+        block_copy(0, step).start()
+
+    for turn in range(1, PLANE):
+        plane_copy(turn).start()
+        block_copy(turn, 0).start()
 
     pl.semaphore_wait(ready_sem, lines - 1)
 
-    def send_rest(first, last):
-        @pl.loop(first, last)
-        def _(turn):
+    def send_rest(turns):
+        for turn in turns:
             @pl.loop(1, lines)
             def _(step):
-                block_copy(turn * lines + step).start()
-
-    send_rest(1, PLANE // 2)
-
-    own = pltpu.make_async_copy(send.at[me], recv.at[pl.ds(me * per, per)], local_sem.at[0])
+                block_copy(turn, lines - step if turn % 2 else step).start()
+
+    send_rest(range(1, PLANE // 2))
+
+    own = pltpu.make_async_copy(send.at[me], arrival(0, line), local_sem.at[0])
     own.start()
     plane_own = pltpu.make_async_copy(plane_send.at[0], plane_recv.at[spot], local_sem.at[1])
     plane_own.start()
@@ -163,7 +172,7 @@
     line_own = pltpu.make_async_copy(line_send.at[0], line_recv.at[line], local_sem.at[2])
     line_own.start()
 
-    send_rest(PLANE // 2, PLANE)
+    send_rest(range(PLANE // 2, PLANE))
 
     own.wait()
     line_own.wait()
@@ -172,26 +181,45 @@
     def _(step):
         line_copy(step).wait()
 
-    to_scalar = pltpu.make_async_copy(line_recv, pairs, local_sem.at[3])
+    partner = line_recv[...]
+    turn_of = (spot + PLANE - (partner // per) % PLANE) % PLANE
+    place = (turn_of * lines + partner // (per * PLANE)) * per + partner % per
+    places[0] = jnp.where(turn_of < EARLY, place, EARLY * lines * per)
+    places[1] = place
+    to_scalar = pltpu.make_async_copy(places, pairs, local_sem.at[3])
     to_scalar.start()
     to_scalar.wait()
 
-    @pl.loop(1, n)
-    def _(step):
-        block_copy(step).wait()
-
-    def add(row, totals):
-        totals = list(totals)
-        for place in range(PLANE):
-            for j in range(per):
-                mine = recv[(row * PLANE + place) * per + j].astype(jnp.float32)
-                for q in range(nq):
-                    at = pairs[row, 0, (place * nq + q) * per + j]
-                    totals[q] = totals[q] + mine * recv[at].astype(jnp.float32)
-        return tuple(totals)
-
-    zero = jnp.zeros(recv.shape[1:], jnp.float32)
-    totals = lax.fori_loop(0, lines, add, (zero,) * nq)
+    zero = jnp.zeros(early.shape[1:], jnp.float32)
+    early[EARLY * lines * per] = zero.astype(early.dtype)
+
+    def wait_for(turns):
+        for turn in turns:
+            @pl.loop(0 if turn else 1, lines)
+            def _(step):
+                block_copy(turn, step).wait()
+
+    def pair_sum(totals, turns, held, table):
+        def add(row, totals):
+            totals = list(totals)
+            for turn in turns:
+                lanes = lax.rem(spot + PLANE - turn, PLANE) * nq * per
+                for j in range(per):
+                    at = (turn * lines + row) * per + j
+                    mine = held[at].astype(jnp.float32)
+                    if held is early:
+                        full[at] = (mine + mine).astype(full.dtype)
+                    for q in range(nq):
+                        other = held[pairs[table, row, 0, lanes + q * per + j]]
+                        totals[q] = totals[q] + mine * other.astype(jnp.float32)
+            return tuple(totals)
+
+        return lax.fori_loop(0, lines, add, totals)
+
+    wait_for(range(EARLY))
+    totals = pair_sum((zero,) * nq, range(EARLY), early, 0)
+    wait_for(range(EARLY, PLANE))
+    totals = pair_sum(totals, range(EARLY, PLANE), full, 1)
     for q in range(nq):
         scaled = totals[q] * (1.0 / (n * per))
         out_ref[:, q, :half] = scaled[:rows]
@@ -221,13 +249,15 @@
                 pltpu.VMEM((npts, npts), bf16),
                 pltpu.VMEM((npts, norb), bf16),
                 pltpu.VMEM((n, per, 2 * rows, npts // 2), bf16),
+                pltpu.VMEM(((EARLY * n // PLANE + 1) * per, 2 * rows, npts // 2), bf16),
                 pltpu.VMEM((n * per, 2 * rows, npts // 2), bf16),
                 pltpu.VMEM((1, 1, LANES), i32),
                 pltpu.VMEM((PLANE, 1, LANES), i32),
                 pltpu.VMEM((1, 1, LANES), i32),
                 pltpu.VMEM((n // PLANE, 1, LANES), i32),
-                pltpu.SMEM((n // PLANE, 1, LANES), i32),
-                dma((5,)),
+                pltpu.VMEM((2, n // PLANE, 1, LANES), i32),
+                pltpu.SMEM((2, n // PLANE, 1, LANES), i32),
+                dma((3 + 2 * per,)),
                 dma((n,)),
                 dma((n,)),
                 dma((PLANE,)),

time: 63 us -> 62.3 us (0.989)
  the two profiles are of different devices: /device:TPU:40 before, /device:TPU:16 now
where the time goes in v6:
time: 62.3 us; the launch traced here: 62.2 us
  Pallas kernels  61.6 us (99%)
    pallas_call x1, Pallas kernels, per_device(): pl.pallas_call(functools.partial(kernel, n), out_shape=jax.ShapeDtypeStru...  61.6 us

profile of v6, /device:TPU:16, one launch (start us, length us, event | category | flops | bytes accessed | tf_op | source)
XLA Modules:
  0.0 62.2 jit_solution(8428899103933783928)
XLA Ops:
  0.0 61.6 %shard_map.55 = f32[8,2,512]{2,1,0:T(2,128)S(1)} custom-call(s32[2]{0:T(128)} %q_hbm.1, bf16[4,256,256]{2,1,0:T(8,128)(2,1)} %green_hbm.1, bf16[4,256,512]{2,1,0:T(8,128)(2,1)} %orb_hbm.1, s32[4,256]{1,0:T(4,128)} %bitcast.2, s32[1,512]{1,0:T(1,128)} %bitcast.3), custom_call_target="tpu_custom_call" | custom-call | flops 1342177280 | bytes 1572864 | tf_op jit(solution)/shard_map/pallas_call | solution.py:238
  61.6 0.6 copy.7

commit v7 on v6

--- a/solution.py
+++ b/solution.py
@@ -15,7 +15,7 @@
 
 def kernel(
     n, q_hbm, green_hbm, orb_hbm, table_hbm, owner_hbm, out_ref,
-    q_ref, green, orb, table, owner, select, owned, send, early, full,
+    q_ref, green, orb, table, owner, owner_columns, select, half_product, send, early, full,
     plane_send, plane_recv, line_send, line_recv, places, pairs,
     load_sem, send_sem, recv_sem, plane_send_sem, plane_recv_sem, line_send_sem, line_recv_sem, local_sem, ready_sem,
 ):
@@ -60,14 +60,85 @@
     for load in small:
         load.wait()
 
-    owner_columns = jnp.transpose(
+    owner_columns[...] = jnp.transpose(
         jnp.broadcast_to(owner[...].astype(jnp.float32), (LANES, npts))
-    )
-    for tile in range(npts // LANES):
-        points = lax.broadcasted_iota(jnp.int32, (npts, LANES), 1) + tile * LANES
-        select[:, tile * LANES : (tile + 1) * LANES] = jnp.where(
-            owner_columns == points.astype(jnp.float32), 1.0, 0.0
-        ).astype(jnp.bfloat16)
+    ).reshape(n, rows, LANES)
+
+    def project(first, last):
+        for turn in range(first, last):
+            place = lax.rem(spot + turn, PLANE)
+            owners = jnp.concatenate([owner_columns[row * PLANE + place] for row in range(lines)], axis=0)
+            for tile in range(npts // LANES):
+                points = lax.broadcasted_iota(jnp.int32, owners.shape, 1) + tile * LANES
+                select[turn * lines * rows : (turn + 1) * lines * rows, tile * LANES : (tile + 1) * LANES] = (
+                    jnp.where(owners == points.astype(jnp.float32), 1.0, 0.0).astype(jnp.bfloat16)
+                )
+        for k in range(per):
+            if first == 0:
+                for load in loads[k]:
+                    load.wait()
+                half_product[k] = jnp.dot(
+                    green[k], orb[k], preferred_element_type=jnp.float32
+                ).astype(jnp.bfloat16)
+            owned = lax.dot_general(
+                select[first * lines * rows : last * lines * rows, :],
+                orb[k],
+                (((1,), (1,)), ((), ())),
+                preferred_element_type=jnp.float32,
+            ).astype(jnp.bfloat16)
+            projected = jnp.dot(owned, half_product[k], preferred_element_type=jnp.float32)
+            projected = projected.reshape((last - first) * lines, rows, npts)
+            send[first * lines : last * lines, k] = jnp.concatenate(
+                [projected[:, :, :half], projected[:, :, half:]], axis=1
+            ).astype(jnp.bfloat16)
+
+    project(0, 1)
+
+    pl.semaphore_wait(barrier, lines - 1 + PLANE - 1)
+
+
+    def arrival(turn, row):
+        place = (turn * lines + row) * per
+        return (early if turn < EARLY else full).at[pl.ds(place, per)]
+
+    def block_copy(turn, step):
+        peer = lax.rem(line + step, lines) * PLANE + lax.rem(spot + turn, PLANE)
+        return pltpu.make_async_remote_copy(
+            src_ref=send.at[turn * lines + lax.rem(line + step, lines)],
+            dst_ref=arrival(turn, line),
+            send_sem=send_sem.at[turn * lines + step],
+            recv_sem=recv_sem.at[turn * lines + step],
+            device_id={"ka": peer},
+            device_id_type=MESH,
+        )
+
+    def plane_copy(step):
+        return pltpu.make_async_remote_copy(
+            src_ref=plane_send.at[0],
+            dst_ref=plane_recv.at[spot],
+            send_sem=plane_send_sem.at[step],
+            recv_sem=plane_recv_sem.at[step],
+            device_id=in_plane(step),
+            device_id_type=MESH,
+        )
+
+    def line_copy(step):
+        return pltpu.make_async_remote_copy(
+            src_ref=line_send.at[0],
+            dst_ref=line_recv.at[line],
+            send_sem=line_send_sem.at[step],
+            recv_sem=line_recv_sem.at[step],
+            device_id=in_line(step),
+            device_id_type=MESH,
+        )
+
+    @pl.loop(1, lines)
+    def _(step):
+        block_copy(0, step).start()
+
+    @pl.loop(1, lines)
+    def _(step):
+        pl.semaphore_signal(ready_sem, inc=1, device_id=in_line(lines - step), device_id_type=MESH)
 
     table_columns = lax.broadcasted_iota(jnp.int32, table.shape, 1)
     lane = lax.broadcasted_iota(jnp.int32, (per, LANES), 1)
@@ -79,70 +150,12 @@
         placed += jnp.where(lane == (spot * nq + q) * per + which, partner, 0)
     plane_send[0] = jnp.sum(placed, axis=0, keepdims=True)
 
-    for k in range(per):
-        for load in loads[k]:
-            load.wait()
-        owned[...] = lax.dot_general(
-            select[...], orb[k], (((1,), (1,)), ((), ())), preferred_element_type=jnp.float32
-        ).astype(jnp.bfloat16)
-        half_product = jnp.dot(
-            green[k], orb[k], preferred_element_type=jnp.float32
-        ).astype(jnp.bfloat16)
-        projected = jnp.dot(owned[...], half_product, preferred_element_type=jnp.float32)
-        projected = projected.reshape(n, rows, npts)
-        send[:, k] = jnp.concatenate(
-            [projected[:, :, :half], projected[:, :, half:]], axis=1
-        ).astype(jnp.bfloat16)
-
-    pl.semaphore_wait(barrier, lines - 1 + PLANE - 1)
-
-    @pl.loop(1, lines)
-    def _(step):
-        pl.semaphore_signal(ready_sem, inc=1, device_id=in_line(lines - step), device_id_type=MESH)
-
-    def arrival(turn, row):
-        place = (turn * lines + row) * per
-        return (early if turn < EARLY else full).at[pl.ds(place, per)]
-
-    def block_copy(turn, step):
-        peer = lax.rem(line + step, lines) * PLANE + lax.rem(spot + turn, PLANE)
-        return pltpu.make_async_remote_copy(
-            src_ref=send.at[peer],
-            dst_ref=arrival(turn, line),
-            send_sem=send_sem.at[turn * lines + step],
-            recv_sem=recv_sem.at[turn * lines + step],
-            device_id={"ka": peer},
-            device_id_type=MESH,
-        )
-
-    def plane_copy(step):
-        return pltpu.make_async_remote_copy(
-            src_ref=plane_send.at[0],
-            dst_ref=plane_recv.at[spot],
-            send_sem=plane_send_sem.at[step],
-            recv_sem=plane_recv_sem.at[step],
-            device_id=in_plane(step),
-            device_id_type=MESH,
-        )
-
-    def line_copy(step):
-        return pltpu.make_async_remote_copy(
-            src_ref=line_send.at[0],
-            dst_ref=line_recv.at[line],
-            send_sem=line_send_sem.at[step],
-            recv_sem=line_recv_sem.at[step],
-            device_id=in_line(step),
-            device_id_type=MESH,
-        )
-
-    @pl.loop(1, lines)
-    def _(step):
-        block_copy(0, step).start()
-
     for turn in range(1, PLANE):
         plane_copy(turn).start()
+
+    project(1, PLANE)
+    for turn in range(1, PLANE):
         block_copy(turn, 0).start()
-
     pl.semaphore_wait(ready_sem, lines - 1)
 
     def send_rest(turns):
@@ -153,7 +166,7 @@
 
     send_rest(range(1, PLANE // 2))
 
-    own = pltpu.make_async_copy(send.at[me], arrival(0, line), local_sem.at[0])
+    own = pltpu.make_async_copy(send.at[line], arrival(0, line), local_sem.at[0])
     own.start()
     plane_own = pltpu.make_async_copy(plane_send.at[0], plane_recv.at[spot], local_sem.at[1])
     plane_own.start()
@@ -246,8 +259,9 @@
                 pltpu.VMEM((per, norb, npts), bf16),
                 pltpu.VMEM((per, n * per), i32),
                 pltpu.VMEM((1, npts), i32),
+                pltpu.VMEM((n, rows, LANES), jnp.float32),
                 pltpu.VMEM((npts, npts), bf16),
-                pltpu.VMEM((npts, norb), bf16),
+                pltpu.VMEM((per, norb, npts), bf16),
                 pltpu.VMEM((n, per, 2 * rows, npts // 2), bf16),
                 pltpu.VMEM(((EARLY * n // PLANE + 1) * per, 2 * rows, npts // 2), bf16),
                 pltpu.VMEM((n * per, 2 * rows, npts // 2), bf16),

time: 62.3 us -> 61.6 us (0.989)
  Pallas kernels: 61.6 us -> 60.8 us
    pallas_call x1, Pallas kernels: 61.6 us -> 60.8 us  [per_device(): pl.pallas_call(functools.partial(kernel, n), out_shape=jax.ShapeDtypeStru...]
where the time goes in v7:
time: 61.6 us; the launch traced here: 61.4 us
  Pallas kernels  60.8 us (99%)
  local copies, waits for them, and re-layouts  0.62 us (1%)
    pallas_call x1, Pallas kernels, per_device(): pl.pallas_call(functools.partial(kernel, n), out_shape=jax.ShapeDtypeStru...  60.8 us

profile of v7, /device:TPU:16, one launch (start us, length us, event | category | flops | bytes accessed | tf_op | source)
XLA Modules:
  0.0 61.4 jit_solution(14017012132271924833)
XLA Ops:
  0.0 60.8 %shard_map.55 = f32[8,2,512]{2,1,0:T(2,128)S(1)} custom-call(s32[2]{0:T(128)} %q_hbm.1, bf16[4,256,256]{2,1,0:T(8,128)(2,1)} %green_hbm.1, bf16[4,256,512]{2,1,0:T(8,128)(2,1)} %orb_hbm.1, s32[4,256]{1,0:T(4,128)} %bitcast.2, s32[1,512]{1,0:T(1,128)} %bitcast.3), custom_call_target="tpu_custom_call" | custom-call | flops 1342177280 | bytes 1572864 | tf_op jit(solution)/shard_map/pallas_call | solution.py:251
  60.8 0.6 %copy.7 = f32[8,2,512]{2,1,0:T(2,128)} copy(f32[8,2,512]{2,1,0:T(2,128)S(1)} %shard_map.55) | data formatting | bytes 65536

commit v8 on v7

--- a/solution.py
+++ b/solution.py
@@ -210,7 +210,7 @@
         for turn in turns:
             @pl.loop(0 if turn else 1, lines)
             def _(step):
-                block_copy(turn, step).wait()
+                block_copy(turn, step).wait_recv()
 
     def pair_sum(totals, turns, held, table):
         def add(row, totals):
@@ -233,6 +233,11 @@
     totals = pair_sum((zero,) * nq, range(EARLY), early, 0)
     wait_for(range(EARLY, PLANE))
     totals = pair_sum(totals, range(EARLY, PLANE), full, 1)
+    for turn in range(PLANE):
+        @pl.loop(0 if turn else 1, lines)
+        def _(step):
+            block_copy(turn, step).wait_send()
+
     for q in range(nq):
         scaled = totals[q] * (1.0 / (n * per))
         out_ref[:, q, :half] = scaled[:rows]

time: 61.6 us -> 62 us (level)
  no operation moved by 1% of the time
where the time goes in v8:
time: 62 us; the launch traced here: 61.8 us
  Pallas kernels  61.2 us (99%)
  local copies, waits for them, and re-layouts  0.62 us (1%)
    pallas_call x1, Pallas kernels, per_device(): pl.pallas_call(functools.partial(kernel, n), out_shape=jax.ShapeDtypeStru...  61.2 us

profile of v8, /device:TPU:16, one launch (start us, length us, event | category | flops | bytes accessed | tf_op | source)
XLA Modules:
  0.0 61.8 jit_solution(15550038231338873599)
XLA Ops:
  0.0 61.2 %shard_map.55 = f32[8,2,512]{2,1,0:T(2,128)S(1)} custom-call(s32[2]{0:T(128)} %q_hbm.1, bf16[4,256,256]{2,1,0:T(8,128)(2,1)} %green_hbm.1, bf16[4,256,512]{2,1,0:T(8,128)(2,1)} %orb_hbm.1, s32[4,256]{1,0:T(4,128)} %bitcast.2, s32[1,512]{1,0:T(1,128)} %bitcast.3), custom_call_target="tpu_custom_call" | custom-call | flops 1342177280 | bytes 1572864 | tf_op jit(solution)/shard_map/pallas_call | solution.py:256
  61.2 0.6 copy.7

commit v9 on v7

--- a/solution.py
+++ b/solution.py
@@ -153,8 +153,8 @@
     for turn in range(1, PLANE):
         plane_copy(turn).start()
 
-    project(1, PLANE)
-    for turn in range(1, PLANE):
+    project(1, PLANE // 2)
+    for turn in range(1, PLANE // 2):
         block_copy(turn, 0).start()
     pl.semaphore_wait(ready_sem, lines - 1)
 
@@ -165,6 +165,9 @@
                 block_copy(turn, lines - step if turn % 2 else step).start()
 
     send_rest(range(1, PLANE // 2))
+    project(PLANE // 2, PLANE)
+    for turn in range(PLANE // 2, PLANE):
+        block_copy(turn, 0).start()
 
     own = pltpu.make_async_copy(send.at[line], arrival(0, line), local_sem.at[0])
     own.start()

time: 61.6 us -> 61.8 us (level)
  the two profiles are of different devices: /device:TPU:16 before, /device:TPU:24 now
where the time goes in v9:
time: 61.8 us; the launch traced here: 61.7 us
  Pallas kernels  61 us (99%)
  local copies, waits for them, and re-layouts  0.62 us (1%)
    pallas_call x1, Pallas kernels, per_device(): pl.pallas_call(functools.partial(kernel, n), out_shape=jax.ShapeDtypeStru...  61 us

profile of v9, /device:TPU:24, one launch (start us, length us, event | category | flops | bytes accessed | tf_op | source)
XLA Modules:
  0.0 61.7 jit_solution(12044179795517771132)
XLA Ops:
  0.0 61.0 %shard_map.55 = f32[8,2,512]{2,1,0:T(2,128)S(1)} custom-call(s32[2]{0:T(128)} %q_hbm.1, bf16[4,256,256]{2,1,0:T(8,128)(2,1)} %green_hbm.1, bf16[4,256,512]{2,1,0:T(8,128)(2,1)} %orb_hbm.1, s32[4,256]{1,0:T(4,128)} %bitcast.2, s32[1,512]{1,0:T(1,128)} %bitcast.3), custom_call_target="tpu_custom_call" | custom-call | flops 1342177280 | bytes 1572864 | tf_op jit(solution)/shard_map/pallas_call | solution.py:254
  61.0 0.6 %copy.7 = f32[8,2,512]{2,1,0:T(2,128)} copy(f32[8,2,512]{2,1,0:T(2,128)S(1)} %shard_map.55) | data formatting | bytes 65536
